TPU v7x, 32 devices: a whole 2x2x4 slice. The times are simulated.
32 devices in a mesh: ex: 8 (over z, x), tp: 4 (over y, core).
Axes of the slice: x: 2, y: 2, z: 4, core: 2. Of those that a mesh axis runs over, the one named last changes fastest.
Arguments:
- inputs: bfloat16 [1024, 768], P('ex'), may hold values from -6 to 6
- routes: int32 [1024, 2], P('ex'), may hold values from 0 to 7, all different within a row; in each aligned block of 128 rows (0 to 127, 128 to 255, ...) at most 64 rows name the same one
- lengths: int32 [8, 4], P('ex'), may hold values from 1 to 96, 128 in all within a row
- w_query: bfloat16 [768, 768], P(None, 'tp'), may hold values from -0.21875 to 0.21875
- w_key: bfloat16 [768, 768], P(None, 'tp'), may hold values from -0.21875 to 0.21875
- w_value: bfloat16 [768, 768], P(None, 'tp'), may hold values from -0.21875 to 0.21875
- w_attn_out: bfloat16 [768, 768], P('tp'), may hold values from -0.875 to 0.875
- gain_attn: float32 [768], replicated, may hold values from 0.25 to 1.75
- gain_moe: float32 [768], replicated, may hold values from 0.25 to 1.75
- rel_bias: float32 [32, 12], P(None, 'tp'), may hold values from -4 to 4
- w_router: bfloat16 [768, 8], replicated, may hold values from -0.15625 to 0.15625
- w_in: bfloat16 [8, 768, 3072], P('ex', None, 'tp'), may hold values from -0.21875 to 0.21875
- w_out: bfloat16 [8, 3072, 768], P('ex', 'tp'), may hold values from -0.109375 to 0.109375
- cotangent: bfloat16 [1024, 768], P('ex'), may hold values from -6 to 6
Outputs:
- output: bfloat16 [1024, 768], P('ex')
- grad_inputs: bfloat16 [1024, 768], P('ex')
- grad_w_query: float32 [768, 768], P(None, 'tp')
- grad_w_key: float32 [768, 768], P(None, 'tp')
- grad_w_value: float32 [768, 768], P(None, 'tp')
- grad_w_attn_out: float32 [768, 768], P('tp')
- grad_gain_attn: float32 [768], replicated
- grad_gain_moe: float32 [768], replicated
- grad_rel_bias: float32 [32, 12], P(None, 'tp')
- grad_w_router: float32 [768, 8], replicated
- grad_w_in: float32 [8, 768, 3072], P('ex', None, 'tp')
- grad_w_out: float32 [8, 3072, 768], P('ex', 'tp')
Inputs may be any that keep to these rules, and one draw needn't show every extreme that they name: `routes`: each row names two different experts. The rows of one index of ex name any one expert at most 64 times, a bound that some block reaches. `lengths`: each row sums to 128 and its largest entry is exactly 96.
All inputs are finite; a program needn't handle non-finite values.
Results may differ from a plain program's by a relative error of at most 0.017.
Values may be sent and summed in bfloat16 or wider, within the bound.
A program may use at most 128 MiB of HBM per device.

v0:
```python
from functools import partial
import math
import jax
import jax.numpy as jnp
from jax import lax
from jax.sharding import PartitionSpec as P

eps = 1e-06
highest = lax.Precision.HIGHEST
bucket_edges = [math.ceil(16 * 8 ** (number / 16)) for number in range(1, 16)]


def rms_scale(values):
    return lax.rsqrt(jnp.mean(values * values, -1, keepdims=True) + eps)


def bucket_of(length):
    positions = jnp.arange(length, dtype=jnp.int32)
    offsets = positions[:, None] - positions[None, :]
    distance = jnp.maximum(offsets, 0)
    counted = jnp.zeros_like(distance)
    for border in bucket_edges:
        counted = counted + (distance >= border).astype(jnp.int32)
    return jnp.where(distance < 16, distance, 16 + counted)


def contract_rows(left_side, right_side):
    return lax.dot_general(
        left_side, right_side, (((0,), (0,)), ((), ())), preferred_element_type=jnp.float32
    )


def contract_cols(left_side, right_side):
    return lax.dot_general(
        left_side, right_side, (((1,), (1,)), ((), ())), preferred_element_type=jnp.float32
    )


def shards(
    inputs,
    routes,
    lengths,
    w_query,
    w_key,
    w_value,
    w_attn_out,
    gain_attn,
    gain_moe,
    rel_bias,
    w_router,
    w_in,
    w_out,
    cotangent,
):
    tok_rows, model_width = inputs.shape
    local_heads = rel_bias.shape[1]
    head_dim = w_query.shape[1] // local_heads
    attn_scale = head_dim ** (-0.5)
    experts = w_router.shape[1]
    ex_devices = lax.axis_size("ex")
    local_experts = w_in.shape[0]
    capacity = 4 * tok_rows // experts
    pair_count = 2 * tok_rows
    inputs_f = inputs.astype(jnp.float32)
    scale_a = rms_scale(inputs_f)
    normed_a = inputs_f * scale_a
    attn_in = (normed_a * gain_attn).astype(jnp.bfloat16)
    query_b = (
        jnp.dot(attn_in, w_query, preferred_element_type=jnp.float32)
        .astype(jnp.bfloat16)
        .reshape(tok_rows, local_heads, head_dim)
    )
    key_b = (
        jnp.dot(attn_in, w_key, preferred_element_type=jnp.float32)
        .astype(jnp.bfloat16)
        .reshape(tok_rows, local_heads, head_dim)
    )
    value_b = (
        jnp.dot(attn_in, w_value, preferred_element_type=jnp.float32)
        .astype(jnp.bfloat16)
        .reshape(tok_rows, local_heads, head_dim)
    )
    buckets = bucket_of(tok_rows)
    one_hot = (
        buckets[None] == jnp.arange(rel_bias.shape[0], dtype=jnp.int32)[:, None, None]
    ).astype(jnp.float32)
    bias_full = jnp.einsum("bij,bh->hij", one_hot, rel_bias, precision=highest)
    seq_ends = jnp.cumsum(lengths[0])
    positions = jnp.arange(tok_rows, dtype=jnp.int32)
    segments = jnp.sum((positions[:, None] >= seq_ends[None, :]).astype(jnp.int32), -1)
    allowed = (segments[:, None] == segments[None, :]) & (positions[:, None] >= positions[None, :])

    def score_of(queries_in, keys_in):
        raw_scores = (
            jnp.einsum("ihd,jhd->hij", queries_in, keys_in, preferred_element_type=jnp.float32)
            * attn_scale
        )
        return jnp.where(allowed[None], raw_scores + bias_full, -1e30)

    scores = score_of(query_b, key_b)
    row_max = jnp.max(scores, -1, keepdims=True)
    log_sum = row_max + jnp.log(jnp.sum(jnp.exp(scores - row_max), -1, keepdims=True))
    probabilities = jnp.exp(scores - log_sum)
    probs_low = probabilities.astype(jnp.bfloat16)
    mixed_heads = (
        jnp.einsum("hij,jhd->ihd", probs_low, value_b, preferred_element_type=jnp.float32)
        .astype(jnp.bfloat16)
        .reshape(tok_rows, -1)
    )
    head_part = jnp.dot(mixed_heads, w_attn_out, preferred_element_type=jnp.float32)
    residual = inputs_f + lax.psum(head_part, "tp")
    scale_m = rms_scale(residual)
    normed_m = residual * scale_m
    moe_in = (normed_m * gain_moe).astype(jnp.bfloat16)
    logits = jnp.dot(moe_in, w_router, preferred_element_type=jnp.float32)
    expert_ids = jnp.arange(experts, dtype=jnp.int32)
    route_hot = (routes[:, :, None] == expert_ids[None, None, :]).astype(jnp.float32)
    chosen_logits = jnp.sum(route_hot * logits[:, None, :], -1)
    gate_max = jnp.max(chosen_logits, -1, keepdims=True)
    gate_exp = jnp.exp(chosen_logits - gate_max)
    gate_values = gate_exp / jnp.sum(gate_exp, -1, keepdims=True)
    pair_routes = routes.reshape(-1)
    pair_hot = (pair_routes[:, None] == expert_ids[None, :]).astype(jnp.int32)
    slot_index = jnp.sum(pair_hot * jnp.cumsum(pair_hot, 0), -1) - 1
    pair_slots = pair_routes * capacity + slot_index
    members = (
        jnp.full((experts * capacity,), pair_count, jnp.int32)
        .at[pair_slots]
        .set(jnp.arange(pair_count, dtype=jnp.int32))
    )
    padded = jnp.concatenate([moe_in, jnp.zeros((1, model_width), jnp.bfloat16)], 0)
    send_rows = padded[members // 2].reshape(experts, capacity, model_width)
    arrived = lax.all_to_all(send_rows, "ex", split_axis=0, concat_axis=0, tiled=True)
    slot_count = arrived.shape[1]
    grouped = arrived.reshape(ex_devices, local_experts, slot_count, model_width)
    pre_act = jnp.einsum("slcd,ldf->slcf", grouped, w_in, preferred_element_type=jnp.float32)
    act_low = jax.nn.gelu(pre_act, approximate=True).astype(jnp.bfloat16)
    partial_out = jnp.einsum("slcf,lfd->slcd", act_low, w_out, preferred_element_type=jnp.float32)
    partial_out = partial_out.reshape(ex_devices * local_experts, slot_count, model_width)
    owned_rows = lax.psum_scatter(
        partial_out.astype(jnp.bfloat16), "tp", scatter_dimension=2, tiled=True
    )
    returned = lax.all_to_all(owned_rows, "ex", split_axis=0, concat_axis=0, tiled=True)
    returned, kept_rows, kept_pre = (
        returned,
        arrived,
        pre_act.reshape(ex_devices * local_experts, slot_count, -1),
    )
    expert_out = lax.all_gather(returned, "tp", axis=2, tiled=True).reshape(
        experts * capacity, model_width
    )
    pair_out = expert_out[pair_slots].reshape(tok_rows, 2, model_width).astype(jnp.float32)
    result = residual + jnp.sum(gate_values[:, :, None] * pair_out, 1)
    output = result.astype(jnp.bfloat16)
    grad_out = cotangent.astype(jnp.float32)
    gate_grad = jnp.sum(grad_out[:, None, :] * pair_out, -1)
    logit_pair = gate_values * (gate_grad - jnp.sum(gate_values * gate_grad, -1, keepdims=True))
    logit_grads = jnp.sum(logit_pair[:, :, None] * route_hot, 1)
    grad_router = jnp.dot(moe_in.astype(jnp.float32).T, logit_grads, precision=highest)
    moe_grad = jnp.dot(logit_grads, w_router.astype(jnp.float32).T, precision=highest)
    pair_grads = (
        (gate_values[:, :, None] * grad_out[:, None, :])
        .astype(jnp.bfloat16)
        .reshape(pair_count, model_width)
    )
    padded_grads = jnp.concatenate([pair_grads, jnp.zeros((1, model_width), jnp.bfloat16)], 0)
    send_grad_rows = padded_grads[members].reshape(experts, capacity, model_width)
    arrived_grads = lax.all_to_all(send_grad_rows, "ex", split_axis=0, concat_axis=0, tiled=True)
    grad_group = arrived_grads.reshape(ex_devices, local_experts, capacity, model_width)
    act_grad = jnp.einsum("slcd,lfd->slcf", grad_group, w_out, preferred_element_type=jnp.float32)
    pre_keep = kept_pre.reshape(ex_devices, local_experts, capacity, -1)
    act_value, gelu_back = jax.vjp(partial(jax.nn.gelu, approximate=True), pre_keep)
    pre_grad = gelu_back(act_grad)[0].astype(jnp.bfloat16)
    act_low = act_value.astype(jnp.bfloat16)
    grad_w_out = jnp.einsum(
        "slcf,slcd->lfd", act_low, grad_group, preferred_element_type=jnp.float32
    )
    rows_group = kept_rows.reshape(ex_devices, local_experts, capacity, model_width)
    grad_w_in = jnp.einsum(
        "slcd,slcf->ldf", rows_group, pre_grad, preferred_element_type=jnp.float32
    )
    row_part = jnp.einsum("slcf,ldf->slcd", pre_grad, w_in, preferred_element_type=jnp.float32)
    row_part = row_part.reshape(ex_devices * local_experts, capacity, model_width)
    row_share = lax.psum_scatter(row_part, "tp", scatter_dimension=2, tiled=True).astype(
        jnp.bfloat16
    )
    row_back = lax.all_to_all(row_share, "ex", split_axis=0, concat_axis=0, tiled=True)
    row_full = lax.all_gather(row_back, "tp", axis=2, tiled=True).reshape(
        experts * capacity, model_width
    )
    moe_grad = moe_grad + jnp.sum(
        row_full[pair_slots].reshape(tok_rows, 2, model_width).astype(jnp.float32), 1
    )
    grad_gain_moe = jnp.sum(moe_grad * normed_m, 0)
    normed_grad_m = moe_grad * gain_moe
    resid_grad = grad_out + scale_m * (
        normed_grad_m - normed_m * jnp.mean(normed_grad_m * normed_m, -1, keepdims=True)
    )
    attn_grad = resid_grad.astype(jnp.bfloat16)
    grad_w_attn_out = contract_rows(mixed_heads, attn_grad)
    mixed_grad = (
        contract_cols(attn_grad, w_attn_out)
        .astype(jnp.bfloat16)
        .reshape(tok_rows, local_heads, head_dim)
    )
    scores_again = score_of(query_b, key_b)
    probs_again = jnp.exp(scores_again - log_sum)
    prob_grad = jnp.einsum("ihd,jhd->hij", mixed_grad, value_b, preferred_element_type=jnp.float32)
    value_grad = jnp.einsum(
        "hij,ihd->jhd",
        probs_again.astype(jnp.bfloat16),
        mixed_grad,
        preferred_element_type=jnp.float32,
    ).astype(jnp.bfloat16)
    score_grad = probs_again * (prob_grad - jnp.sum(probs_again * prob_grad, -1, keepdims=True))
    grad_rel_bias = jnp.einsum("hij,bij->bh", score_grad, one_hot, precision=highest)
    score_low = score_grad.astype(jnp.bfloat16)
    query_grad = (
        (
            jnp.einsum("hij,jhd->ihd", score_low, key_b, preferred_element_type=jnp.float32)
            * attn_scale
        )
        .astype(jnp.bfloat16)
        .reshape(tok_rows, -1)
    )
    key_grad = (
        (
            jnp.einsum("hij,ihd->jhd", score_low, query_b, preferred_element_type=jnp.float32)
            * attn_scale
        )
        .astype(jnp.bfloat16)
        .reshape(tok_rows, -1)
    )
    value_flat = value_grad.reshape(tok_rows, -1)
    grad_w_query = contract_rows(attn_in, query_grad)
    grad_w_key = contract_rows(attn_in, key_grad)
    grad_w_value = contract_rows(attn_in, value_flat)
    input_part = (
        contract_cols(query_grad, w_query)
        + contract_cols(key_grad, w_key)
        + contract_cols(value_flat, w_value)
    )
    input_grad = lax.psum(input_part.astype(jnp.bfloat16), "tp").astype(jnp.float32)
    grad_gain_attn = jnp.sum(input_grad * normed_a, 0)
    normed_grad_a = input_grad * gain_attn
    grad_inputs = (
        resid_grad
        + scale_a
        * (normed_grad_a - normed_a * jnp.mean(normed_grad_a * normed_a, -1, keepdims=True))
    ).astype(jnp.bfloat16)
    dense_sums = lax.psum(
        (
            grad_w_query,
            grad_w_key,
            grad_w_value,
            grad_w_attn_out,
            grad_gain_attn,
            grad_gain_moe,
            grad_rel_bias,
            grad_router,
        ),
        "ex",
    )
    return (
        output,
        grad_inputs,
        dense_sums[0],
        dense_sums[1],
        dense_sums[2],
        dense_sums[3],
        dense_sums[4],
        dense_sums[5],
        dense_sums[6],
        dense_sums[7],
        grad_w_in,
        grad_w_out,
    )


def solution(mesh):
    placed = (
        P("ex", None),
        P("ex", None),
        P("ex", None),
        P(None, "tp"),
        P(None, "tp"),
        P(None, "tp"),
        P("tp", None),
        P(),
        P(),
        P(None, "tp"),
        P(),
        P("ex", None, "tp"),
        P("ex", "tp", None),
        P("ex", None),
    )
    return jax.shard_map(
        shards,
        mesh=mesh,
        in_specs=placed,
        out_specs=(
            P("ex", None),
            P("ex", None),
            P(None, "tp"),
            P(None, "tp"),
            P(None, "tp"),
            P("tp", None),
            P(),
            P(),
            P(None, "tp"),
            P(),
            P("ex", None, "tp"),
            P("ex", "tp", None),
        ),
        check_vma=False,
    )
```

profile of v0, /device:TPU:0, one launch (start us, length us, event | category | flops | bytes accessed | tf_op | source)
XLA Modules:
  0.0 362.4 jit_solution(3472108545965280200)
XLA Ops:
  18.6 31.8 %all-reduce.8.cloned.1.call-done = f32[128,768]{1,0:T(8,128)} async-done(((f32[128,768]{1,0:T(8,128)}), f32[128,768]{1,0:T(8,128)}) %all-reduce.8.cloned.1.call-update) | async-done | bytes 393232 | tf_op jit(solution)/shard_map/psum | solution.py:111
  52.9 2.7 gather_fusion
  55.6 5.6 %all-to-all-start = ((bf16[8,64,768]{2,1,0:T(8,128)(2,1)}), bf16[8,64,768]{2,1,0:T(8,128)(2,1)}, u32[]{:S(2)}, u32[]{:S(2)}) async-start(bf16[8,64,768]{2,1,0:T(8,128)(2,1)} %bitcast.13), calls=%async_computation | async-start | bytes 1572864 | tf_op jit(solution)/shard_map/all_to_all | solution.py:133
  65.4 2.7 gather_fusion.2
  68.1 12.4 %all-to-all-done = bf16[8,64,768]{2,1,0:T(8,128)(2,1)} async-done(((bf16[8,64,768]{2,1,0:T(8,128)(2,1)}), bf16[8,64,768]{2,1,0:T(8,128)(2,1)}, u32[]{:S(2)}, u32[]{:S(2)}) %all-to-all-start) | async-done | bytes 786464 | tf_op jit(solution)/shard_map/all_to_all | solution.py:133
  80.5 4.3 %all-to-all-start.2 = ((bf16[8,64,768]{2,1,0:T(8,128)(2,1)}), bf16[8,64,768]{2,1,0:T(8,128)(2,1)}, u32[]{:S(2)}, u32[]{:S(2)}) async-start(bf16[8,64,768]{2,1,0:T(8,128)(2,1)} %bitcast.25), calls=%async_computation.2 | async-start | bytes 1572864 | tf_op jit(solution)/shard_map/all_to_all | solution.py:168
  84.9 1.9 fusion.18
  87.9 1.9 convolution_convert_fusion
  89.9 2.0 copy.96
  93.9 10.5 %all-to-all-done.2 = bf16[8,64,768]{2,1,0:T(8,128)(2,1)} async-done(((bf16[8,64,768]{2,1,0:T(8,128)(2,1)}), bf16[8,64,768]{2,1,0:T(8,128)(2,1)}, u32[]{:S(2)}, u32[]{:S(2)}) %all-to-all-start.2) | async-done | bytes 786464 | tf_op jit(solution)/shard_map/all_to_all | solution.py:168
  104.4 3.1 fusion.13
  108.4 2.1 fusion.16
  110.5 2.3 copy.98
  112.7 3.7 %reshape.492 = f32[768,512]{1,0:T(8,128)} reshape(f32[768,8,64]{2,1,0:T(8,128)} %bitcast.149) | data formatting | bytes 3145728
  120.1 5.5 %all-to-all-start.1 = ((bf16[8,64,192]{2,1,0:T(8,128)(2,1)}), bf16[8,64,192]{2,1,0:T(8,128)(2,1)S(1)}, u32[]{:S(2)}, u32[]{:S(2)}) async-start(bf16[8,64,192]{2,1,0:T(8,128)(2,1)} %copy.97), calls=%async_computation.1 | async-start | bytes 524288 | tf_op jit(solution)/shard_map/all_to_all | solution.py:143
  126.4 8.1 %all-to-all-done.1 = bf16[8,64,192]{2,1,0:T(8,128)(2,1)S(1)} async-done(((bf16[8,64,192]{2,1,0:T(8,128)(2,1)}), bf16[8,64,192]{2,1,0:T(8,128)(2,1)S(1)}, u32[]{:S(2)}, u32[]{:S(2)}) %all-to-all-start.1) | async-done | bytes 196640 | tf_op jit(solution)/shard_map/all_to_all | solution.py:143
  134.8 20.2 %all_gather.6 = bf16[8,64,768]{1,0,2:T(8,128)(2,1)} all-gather(bf16[8,64,192]{1,0,2:T(8,128)(2,1)S(1)} %copy.81), channel_id=1, replica_groups=mesh['ex'=8,'tp'=4] {'tp'}, dimensions={2}, use_global_device_ids=true | all-gather | bytes 983040 | tf_op jit(solution)/shard_map/all_gather | solution.py:149
  154.9 2.0 copy.82
  158.6 2.4 multiply_reduce_fusion
  163.3 3.4 all-to-all-start.3
  166.8 9.5 %all-to-all-done.3 = bf16[8,64,192]{2,1,0:T(8,128)(2,1)S(1)} async-done(((bf16[8,64,192]{2,1,0:T(8,128)(2,1)}), bf16[8,64,192]{2,1,0:T(8,128)(2,1)S(1)}, u32[]{:S(2)}, u32[]{:S(2)}) %all-to-all-start.3) | async-done | bytes 196640 | tf_op jit(solution)/shard_map/all_to_all | solution.py:187
  176.6 13.6 %all_gather.7 = bf16[8,64,768]{1,0,2:T(8,128)(2,1)} all-gather(bf16[8,64,192]{1,0,2:T(8,128)(2,1)S(1)} %copy.86), channel_id=1, replica_groups=mesh['ex'=8,'tp'=4] {'tp'}, dimensions={2}, use_global_device_ids=true | all-gather | bytes 983040 | tf_op jit(solution)/shard_map/all_gather | solution.py:188
  190.2 2.0 copy.87
  192.2 1.9 gather_fusion.3
  195.5 1.7 reduce_sum.164
  206.7 3.5 convolution_bitcast_fusion.1
  210.2 3.5 convolution_bitcast_fusion
  215.2 21.0 %all-reduce.10.cloned.1.call-done = bf16[128,768]{1,0:T(8,128)(2,1)} async-done(((bf16[128,768]{1,0:T(8,128)(2,1)}), bf16[128,768]{1,0:T(8,128)(2,1)}) %all-reduce.10.cloned.1.call-update) | async-done | bytes 196624 | tf_op jit(solution)/shard_map/psum | solution.py:243
  237.4 40.3 %all-reduce.2 = (f32[768]{0:T(1024)}, f32[768]{0:T(1024)}, f32[32,3]{0,1:T(4,128)}, f32[768,8]{0,1:T(8,128)}) all-reduce(f32[768]{0:T(1024)S(1)} %get-tuple-element.16, f32[768]{0:T(1024)S(1)} %get-tuple-element.12, f32[32,3]{0,1:T(4,128)S(1)} %fusion.25, f32[768,8]{0,1:T(8,128)S(1)} %fusion.98), channel_id=1, replica_groups=mesh['ex'=8,'tp'=4] {'ex'}, use_global_device_ids=true, to_apply=%region_30.31 | all-reduce | flops 7776 | bytes 62208 | tf_op jit(solution)/shard_map/psum | solution.py:251
  277.6 1.8 fusion.37
  279.4 71.9 %all-reduce.12.cloned.1.call-done = (f32[768,192]{0,1:T(8,128)}, f32[768,192]{0,1:T(8,128)}, f32[768,192]{0,1:T(8,128)}, f32[192,768]{1,0:T(8,128)}) async-done(((f32[768,192]{0,1:T(8,128)}, f32[768,192]{0,1:T(8,128)}, f32[768,192]{0,1:T(8,128)}, f32[192,768]{1,0:T(8,128)}), (f32[768,192]{0,1:T(8,128)}, f32[768,192]{0,1:T(8,128)}, f32[768,192]{0,1:T(8,128)}, ...) | async-done | bytes 2359312 | tf_op jit(solution)/shard_map/psum | solution.py:251
  351.4 2.0 copy.106
  (201 shorter events, 46.1 us)
Async XLA Ops:
  7.2 80.8 %copy-start = (bf16[1,768,768]{2,1,0:T(8,128)(2,1)S(1)}, bf16[1,768,768]{2,1,0:T(8,128)(2,1)}, u32[]{:S(2)}) copy-start(bf16[1,768,768]{2,1,0:T(8,128)(2,1)} %param.26) | copy-start | bytes 3538948
  7.2 4.5 %copy-start.1 = (bf16[128,768]{1,0:T(8,128)(2,1)S(1)}, bf16[128,768]{1,0:T(8,128)(2,1)}, u32[]{:S(2)}) copy-start(bf16[128,768]{1,0:T(8,128)(2,1)} %param.14) | copy-start | bytes 589828
  7.2 4.5 %copy-start.26 = (f32[768]{0:T(1024)S(1)}, f32[768]{0:T(1024)}, u32[]{:S(2)}) copy-start(f32[768]{0:T(1024)} %param.21) | copy-start | bytes 9220
  7.2 4.5 %copy-start.16 = (bf16[768,192]{0,1:T(8,128)(2,1)S(1)}, bf16[768,192]{0,1:T(8,128)(2,1)}, u32[]{:S(2)}) copy-start(bf16[768,192]{0,1:T(8,128)(2,1)} %param.17) | copy-start | bytes 884740
  7.2 4.8 %copy-start.18 = (bf16[768,192]{0,1:T(8,128)(2,1)S(1)}, bf16[768,192]{0,1:T(8,128)(2,1)}, u32[]{:S(2)}) copy-start(bf16[768,192]{0,1:T(8,128)(2,1)} %param.18) | copy-start | bytes 884740
  7.2 5.1 %copy-start.45 = (s32[1,4]{1,0:T(1,128)S(1)}, s32[1,4]{1,0:T(1,128)}, u32[]{:S(2)}) copy-start(s32[1,4]{1,0:T(1,128)} %param.16) | copy-start | bytes 52
  7.3 43.1 %all-reduce.8.cloned.1.call-start = ((), (), s32[]{:S(2)}) async-start(), calls=%async_computation.6 | async-start | bytes 786432 | tf_op jit(solution)/shard_map/psum | solution.py:111
  7.4 5.3 %copy-start.27 = (s32[128,128]{1,0:T(8,128)}, s32[128,128]{1,0:T(8,128)S(1)}, u32[]{:S(2)}) copy-start(s32[128,128]{1,0:T(8,128)S(1)} %compare_select_fusion) | copy-start | bytes 196612
  8.7 4.1 %copy-start.35 = (f32[128]{0:T(128)}, f32[128]{0:T(128)S(1)}, u32[]{:S(2)}) copy-start(f32[128]{0:T(128)S(1)} %add_rsqrt_fusion.1) | copy-start | bytes 1540
  10.1 3.8 %copy-start.6 = (bf16[192,768]{1,0:T(8,128)(2,1)S(1)}, bf16[192,768]{1,0:T(8,128)(2,1)}, u32[]{:S(2)}) copy-start(bf16[192,768]{1,0:T(8,128)(2,1)} %param.20) | copy-start | bytes 884740
  12.0 4.1 %copy-start.20 = (bf16[128,192]{0,1:T(8,128)(2,1)}, bf16[128,192]{0,1:T(8,128)(2,1)S(1)}, u32[]{:S(2)}) copy-start(bf16[128,192]{0,1:T(8,128)(2,1)S(1)} %convolution_convert_fusion.5) | copy-start | bytes 147460
  12.4 39.1 %copy-start.22 = (bf16[128,192]{0,1:T(8,128)(2,1)}, bf16[128,192]{0,1:T(8,128)(2,1)S(1)}, u32[]{:S(2)}) copy-start(bf16[128,192]{0,1:T(8,128)(2,1)S(1)} %convolution_convert_fusion.4) | copy-start | bytes 147460
  13.0 39.0 %copy-start.30 = (f32[768]{0:T(1024)S(1)}, f32[768]{0:T(1024)}, u32[]{:S(2)}) copy-start(f32[768]{0:T(1024)} %param.22) | copy-start | bytes 9220
  55.6 5.6 %copy-start.4 = (bf16[128,768]{1,0:T(8,128)(2,1)S(1)}, bf16[128,768]{1,0:T(8,128)(2,1)}, u32[]{:S(2)}) copy-start(bf16[128,768]{1,0:T(8,128)(2,1)} %param.27) | copy-start | bytes 589828
  55.6 24.9 %all-to-all-start = ((bf16[8,64,768]{2,1,0:T(8,128)(2,1)}), bf16[8,64,768]{2,1,0:T(8,128)(2,1)}, u32[]{:S(2)}, u32[]{:S(2)}) async-start(bf16[8,64,768]{2,1,0:T(8,128)(2,1)} %bitcast.13), calls=%async_computation | async-start | bytes 1572864 | tf_op jit(solution)/shard_map/all_to_all | solution.py:133
  80.5 4.4 %copy-start.44 = (bf16[1,768,768]{2,1,0:T(8,128)(2,1)S(1)}, bf16[1,768,768]{2,1,0:T(8,128)(2,1)}, u32[]{:S(2)}) copy-start(bf16[1,768,768]{2,1,0:T(8,128)(2,1)} %param.25) | copy-start | bytes 3538948
  80.5 23.9 %all-to-all-start.2 = ((bf16[8,64,768]{2,1,0:T(8,128)(2,1)}), bf16[8,64,768]{2,1,0:T(8,128)(2,1)}, u32[]{:S(2)}, u32[]{:S(2)}) async-start(bf16[8,64,768]{2,1,0:T(8,128)(2,1)} %bitcast.25), calls=%async_computation.2 | async-start | bytes 1572864 | tf_op jit(solution)/shard_map/all_to_all | solution.py:168
  84.8 33.1 %reduce-scatter.7.cloned.1.call-start = ((), (), s32[]{:S(2)}) async-start(), calls=%async_computation.8 | async-start | bytes 983040
  93.6 67.4 %reduce-scatter.9.cloned.1.call-start = ((), (), s32[]{:S(2)}) async-start(), calls=%async_computation.9 | async-start | bytes 1966080
  116.5 9.1 %copy-start.5 = (bf16[128,768]{1,0:T(8,128)(2,1)S(1)}, bf16[128,768]{1,0:T(8,128)(2,1)}, u32[]{:S(2)}) copy-start(bf16[128,768]{1,0:T(8,128)(2,1)} %param.27) | copy-start | bytes 589828
  116.5 9.9 %copy-start.43 = (s32[256,1]{0,1:T(1,128)S(1)}, s32[256,1]{0,1:T(1,128)}, u32[]{:S(2)}) copy-start(s32[256,1]{0,1:T(1,128)} %copy-done.42) | copy-start | bytes 3076
  120.1 14.4 %all-to-all-start.1 = ((bf16[8,64,192]{2,1,0:T(8,128)(2,1)}), bf16[8,64,192]{2,1,0:T(8,128)(2,1)S(1)}, u32[]{:S(2)}, u32[]{:S(2)}) async-start(bf16[8,64,192]{2,1,0:T(8,128)(2,1)} %copy.97), calls=%async_computation.1 | async-start | bytes 524288 | tf_op jit(solution)/shard_map/all_to_all | solution.py:143
  158.6 8.2 %copy-start.34 = (f32[128]{0:T(128)S(1)}, f32[128]{0:T(128)}, u32[]{:S(2)}) copy-start(f32[128]{0:T(128)} %copy-done.33) | copy-start | bytes 1540
  158.6 8.2 %copy-start.39 = (f32[128]{0:T(128)S(1)}, f32[128]{0:T(128)}, u32[]{:S(2)}) copy-start(f32[128]{0:T(128)} %copy-done.38) | copy-start | bytes 1540
  158.6 8.2 %copy-start.32 = (s32[128,2]{0,1:T(2,128)S(1)}, s32[128,2]{0,1:T(2,128)}, u32[]{:S(2)}) copy-start(s32[128,2]{0,1:T(2,128)} %param.15) | copy-start | bytes 3076
  163.3 13.1 %all-to-all-start.3 = ((bf16[8,64,192]{2,1,0:T(8,128)(2,1)}), bf16[8,64,192]{2,1,0:T(8,128)(2,1)S(1)}, u32[]{:S(2)}, u32[]{:S(2)}) async-start(bf16[8,64,192]{2,1,0:T(8,128)(2,1)} %copy.99), calls=%async_computation.3 | async-start | bytes 524288 | tf_op jit(solution)/shard_map/all_to_all | solution.py:187
  166.7 69.5 %all-reduce.10.cloned.1.call-start = ((), (), s32[]{:S(2)}) async-start(), calls=%async_computation.7 | async-start | bytes 393216 | tf_op jit(solution)/shard_map/psum | solution.py:243
  200.8 3.5 copy-start.19
  205.5 145.8 %all-reduce.12.cloned.1.call-start = ((), (), s32[]{:S(2)}) async-start(), calls=%async_computation.10 | async-start | bytes 4718592 | tf_op jit(solution)/shard_map/psum | solution.py:251
  210.2 3.5 copy-start.3
  210.2 3.9 %copy-start.28 = (s32[128,128]{1,0:T(8,128)S(1)}, s32[128,128]{1,0:T(8,128)}, u32[]{:S(2)}) copy-start(s32[128,128]{1,0:T(8,128)} %copy-done.27) | copy-start | bytes 196612
  351.4 3.7 %copy-start.8 = (f32[192,768]{1,0:T(8,128)S(1)}, f32[192,768]{1,0:T(8,128)}, u32[]{:S(2)}) copy-start(f32[192,768]{1,0:T(8,128)} %get-tuple-element.44) | copy-start | bytes 1769476
  (27 other events, 50.6 us)
Sparse Core Ops, SparseCore 0:
  15.0 35.3 all-reduce.7
  93.7 24.1 reduce-scatter.6
  121.0 34.1 reduce-scatter.8
  205.6 30.5 all-reduce.9
  240.5 110.7 all-reduce.11
where the time goes:
time: 364 us; the launch traced here: 362 us
  waiting for transfers between devices  167 us (46%)
  blocking collectives  74 us (20%)
  local copies, waits for them, and re-layouts  42.2 us (12%)
  matrix products  31.6 us (9%)
  starting transfers between devices  19.3 us (5%)
  between operations  14.6 us (4%)
  other arithmetic  14 us (4%)
    psum x1, waiting for transfers between devices, shards(): lax.psum((grad_w_query, grad_w_key, grad_w_value, grad_w_attn_out, grad_g...  71.9 us
    psum x1, blocking collectives, shards(): lax.psum((grad_w_query, grad_w_key, grad_w_value, grad_w_attn_out, grad_g...  40.3 us
    psum x1, waiting for transfers between devices, shards(): residual = inputs_f + lax.psum(head_part, 'tp')  31.8 us
    unnamed x113, local copies, waits for them, and re-layouts  23.8 us
    psum x1, waiting for transfers between devices, shards(): lax.psum(input_part.astype(jnp.bfloat16), 'tp').astype(jnp.float32)  21 us
    all_gather x1, blocking collectives, shards(): lax.all_gather(returned, 'tp', axis=2, tiled=True)  20.2 us
    all_gather x1, blocking collectives, shards(): lax.all_gather(row_back, 'tp', axis=2, tiled=True)  13.6 us
    all_to_all x1, waiting for transfers between devices, shards(): lax.all_to_all(send_rows, 'ex', split_axis=0, concat_axis=0, tiled=True)  12.4 us
  transfers between devices with their start and end apart: 9, of which 8 were waited for; matrix products, arithmetic and copies ran while one was open for 14% of the time, Pallas kernels for 0%

commit v1 on v0

--- a/solution.py
+++ b/solution.py
@@ -108,7 +108,7 @@
         .reshape(tok_rows, -1)
     )
     head_part = jnp.dot(mixed_heads, w_attn_out, preferred_element_type=jnp.float32)
-    residual = inputs_f + lax.psum(head_part, "tp")
+    residual = inputs_f + jnp.sum(lax.all_gather(head_part, "tp"), axis=0)
     scale_m = rms_scale(residual)
     normed_m = residual * scale_m
     moe_in = (normed_m * gain_moe).astype(jnp.bfloat16)

time: 364 us -> 352 us (0.967)
  waiting for transfers between devices: 167 us -> 155 us
    psum x1 -> x0, waiting for transfers between devices: 31.8 us -> none  [shards(): residual = inputs_f + lax.psum(head_part, 'tp')]
    all_gather x0 -> x1, waiting for transfers between devices: none -> 18.8 us  [shards(): residual = inputs_f + jnp.sum(lax.all_gather(head_part, 'tp'), axis=0)]
where the time goes in v1:
time: 352 us; the launch traced here: 351 us
  waiting for transfers between devices  155 us (44%)
  blocking collectives  73.7 us (21%)
  local copies, waits for them, and re-layouts  42.2 us (12%)
  matrix products  31.5 us (9%)
  starting transfers between devices  19.3 us (5%)
  other arithmetic  14.6 us (4%)
  between operations  14.6 us (4%)
    psum x1, waiting for transfers between devices, shards(): lax.psum((grad_w_query, grad_w_key, grad_w_value, grad_w_attn_out, grad_g...  72.7 us
    psum x1, blocking collectives, shards(): lax.psum((grad_w_query, grad_w_key, grad_w_value, grad_w_attn_out, grad_g...  40.1 us
    unnamed x113, local copies, waits for them, and re-layouts  23.8 us
    psum x1, waiting for transfers between devices, shards(): lax.psum(input_part.astype(jnp.bfloat16), 'tp').astype(jnp.float32)  21 us
    all_gather x1, blocking collectives, shards(): lax.all_gather(returned, 'tp', axis=2, tiled=True)  20 us
    all_gather x1, waiting for transfers between devices, shards(): residual = inputs_f + jnp.sum(lax.all_gather(head_part, 'tp'), axis=0)  18.8 us
    all_to_all x1, waiting for transfers between devices, shards(): lax.all_to_all(send_rows, 'ex', split_axis=0, concat_axis=0, tiled=True)  13.8 us
    all_gather x1, blocking collectives, shards(): lax.all_gather(row_back, 'tp', axis=2, tiled=True)  13.7 us
  transfers between devices with their start and end apart: 9, of which 8 were waited for; matrix products, arithmetic and copies ran while one was open for 14% of the time, Pallas kernels for 0%

profile of v1, /device:TPU:0, one launch (start us, length us, event | category | flops | bytes accessed | tf_op | source)
XLA Modules:
  0.0 351.3 jit_solution(8533961253590650615)
XLA Ops:
  18.6 18.8 %all-gather.3.cloned.1.call-done = f32[512,768]{1,0:T(8,128)} async-done(((f32[128,768]{1,0:T(8,128)}), f32[512,768]{1,0:T(8,128)}) %all-gather.3.cloned.1.call-update) | async-done | bytes 1572880 | tf_op jit(solution)/shard_map/all_gather | solution.py:111
  40.4 2.7 gather_fusion
  43.1 5.6 %all-to-all-start = ((bf16[8,64,768]{2,1,0:T(8,128)(2,1)}), bf16[8,64,768]{2,1,0:T(8,128)(2,1)}, u32[]{:S(2)}, u32[]{:S(2)}) async-start(bf16[8,64,768]{2,1,0:T(8,128)(2,1)} %bitcast.14), calls=%async_computation | async-start | bytes 1572864 | tf_op jit(solution)/shard_map/all_to_all | solution.py:133
  52.9 2.7 gather_fusion.2
  55.7 13.8 %all-to-all-done = bf16[8,64,768]{2,1,0:T(8,128)(2,1)} async-done(((bf16[8,64,768]{2,1,0:T(8,128)(2,1)}), bf16[8,64,768]{2,1,0:T(8,128)(2,1)}, u32[]{:S(2)}, u32[]{:S(2)}) %all-to-all-start) | async-done | bytes 786464 | tf_op jit(solution)/shard_map/all_to_all | solution.py:133
  69.4 4.3 %all-to-all-start.2 = ((bf16[8,64,768]{2,1,0:T(8,128)(2,1)}), bf16[8,64,768]{2,1,0:T(8,128)(2,1)}, u32[]{:S(2)}, u32[]{:S(2)}) async-start(bf16[8,64,768]{2,1,0:T(8,128)(2,1)} %bitcast.26), calls=%async_computation.2 | async-start | bytes 1572864 | tf_op jit(solution)/shard_map/all_to_all | solution.py:168
  73.9 1.9 fusion.18
  76.9 1.9 convolution_convert_fusion
  78.9 2.0 copy.96
  82.8 10.9 %all-to-all-done.2 = bf16[8,64,768]{2,1,0:T(8,128)(2,1)} async-done(((bf16[8,64,768]{2,1,0:T(8,128)(2,1)}), bf16[8,64,768]{2,1,0:T(8,128)(2,1)}, u32[]{:S(2)}, u32[]{:S(2)}) %all-to-all-start.2) | async-done | bytes 786464 | tf_op jit(solution)/shard_map/all_to_all | solution.py:168
  93.7 3.1 fusion.13
  97.8 2.1 fusion.16
  99.9 2.3 copy.98
  102.1 3.7 %reshape.493 = f32[768,512]{1,0:T(8,128)} reshape(f32[768,8,64]{2,1,0:T(8,128)} %bitcast.150) | data formatting | bytes 3145728
  108.5 5.5 %all-to-all-start.1 = ((bf16[8,64,192]{2,1,0:T(8,128)(2,1)}), bf16[8,64,192]{2,1,0:T(8,128)(2,1)S(1)}, u32[]{:S(2)}, u32[]{:S(2)}) async-start(bf16[8,64,192]{2,1,0:T(8,128)(2,1)} %copy.97), calls=%async_computation.1 | async-start | bytes 524288 | tf_op jit(solution)/shard_map/all_to_all | solution.py:143
  114.8 8.1 %all-to-all-done.1 = bf16[8,64,192]{2,1,0:T(8,128)(2,1)S(1)} async-done(((bf16[8,64,192]{2,1,0:T(8,128)(2,1)}), bf16[8,64,192]{2,1,0:T(8,128)(2,1)S(1)}, u32[]{:S(2)}, u32[]{:S(2)}) %all-to-all-start.1) | async-done | bytes 196640 | tf_op jit(solution)/shard_map/all_to_all | solution.py:143
  123.2 20.0 %all_gather.14 = bf16[8,64,768]{1,0,2:T(8,128)(2,1)} all-gather(bf16[8,64,192]{1,0,2:T(8,128)(2,1)S(1)} %copy.81), channel_id=1, replica_groups=mesh['ex'=8,'tp'=4] {'tp'}, dimensions={2}, use_global_device_ids=true | all-gather | bytes 983040 | tf_op jit(solution)/shard_map/all_gather | solution.py:149
  143.1 2.0 copy.82
  146.8 2.4 multiply_reduce_fusion
  151.5 3.4 all-to-all-start.3
  155.1 9.5 %all-to-all-done.3 = bf16[8,64,192]{2,1,0:T(8,128)(2,1)S(1)} async-done(((bf16[8,64,192]{2,1,0:T(8,128)(2,1)}), bf16[8,64,192]{2,1,0:T(8,128)(2,1)S(1)}, u32[]{:S(2)}, u32[]{:S(2)}) %all-to-all-start.3) | async-done | bytes 196640 | tf_op jit(solution)/shard_map/all_to_all | solution.py:187
  164.8 13.7 %all_gather.15 = bf16[8,64,768]{1,0,2:T(8,128)(2,1)} all-gather(bf16[8,64,192]{1,0,2:T(8,128)(2,1)S(1)} %copy.86), channel_id=1, replica_groups=mesh['ex'=8,'tp'=4] {'tp'}, dimensions={2}, use_global_device_ids=true | all-gather | bytes 983040 | tf_op jit(solution)/shard_map/all_gather | solution.py:188
  178.5 2.0 copy.87
  180.6 1.9 gather_fusion.3
  183.9 1.7 reduce_sum.174
  195.1 3.5 convolution_bitcast_fusion.1
  198.6 3.5 %convolution_bitcast_fusion = f32[1,768,768]{2,1,0:T(8,128)} fusion(bf16[8,64,768]{2,1,0:T(8,128)(2,1)} %all-to-all-done.2, f32[8,64,768]{2,1,0:T(8,128)S(1)} %copy-done.47), kind=kOutput, calls=%fused_computation.10 | convolution fusion | flops 607518720 | bytes 4718592 | tf_op jit(solution)/shard_map/slcf,slcd->lfd/dot_general | solution.py:175
  203.5 21.0 %all-reduce.7.cloned.1.call-done = bf16[128,768]{1,0:T(8,128)(2,1)} async-done(((bf16[128,768]{1,0:T(8,128)(2,1)}), bf16[128,768]{1,0:T(8,128)(2,1)}) %all-reduce.7.cloned.1.call-update) | async-done | bytes 196624 | tf_op jit(solution)/shard_map/psum | solution.py:243
  225.7 40.1 %all-reduce.2 = (f32[768]{0:T(1024)}, f32[768]{0:T(1024)}, f32[32,3]{0,1:T(4,128)}, f32[768,8]{0,1:T(8,128)}) all-reduce(f32[768]{0:T(1024)S(1)} %get-tuple-element.16, f32[768]{0:T(1024)S(1)} %get-tuple-element.12, f32[32,3]{0,1:T(4,128)S(1)} %fusion.25, f32[768,8]{0,1:T(8,128)S(1)} %fusion.98), channel_id=1, replica_groups=mesh['ex'=8,'tp'=4] {'ex'}, use_global_device_ids=true, to_apply=%region_30.31 | all-reduce | flops 7776 | bytes 62208 | tf_op jit(solution)/shard_map/psum | solution.py:251
  265.8 1.8 fusion.37
  267.6 72.7 %all-reduce.9.cloned.1.call-done = (f32[768,192]{0,1:T(8,128)}, f32[768,192]{0,1:T(8,128)}, f32[768,192]{0,1:T(8,128)}, f32[192,768]{1,0:T(8,128)}) async-done(((f32[768,192]{0,1:T(8,128)}, f32[768,192]{0,1:T(8,128)}, f32[768,192]{0,1:T(8,128)}, f32[192,768]{1,0:T(8,128)}), (f32[768,192]{0,1:T(8,128)}, f32[768,192]{0,1:T(8,128)}, f32[768,192]{0,1:T(8,128)}, ...) | async-done | bytes 2359312 | tf_op jit(solution)/shard_map/psum | solution.py:251
  340.3 2.0 copy.105
  (202 shorter events, 45.7 us)
Async XLA Ops:
  7.2 69.7 %copy-start = (bf16[1,768,768]{2,1,0:T(8,128)(2,1)S(1)}, bf16[1,768,768]{2,1,0:T(8,128)(2,1)}, u32[]{:S(2)}) copy-start(bf16[1,768,768]{2,1,0:T(8,128)(2,1)} %param.26) | copy-start | bytes 3538948
  7.2 4.5 %copy-start.1 = (bf16[128,768]{1,0:T(8,128)(2,1)S(1)}, bf16[128,768]{1,0:T(8,128)(2,1)}, u32[]{:S(2)}) copy-start(bf16[128,768]{1,0:T(8,128)(2,1)} %param.14) | copy-start | bytes 589828
  7.2 4.5 %copy-start.26 = (f32[768]{0:T(1024)S(1)}, f32[768]{0:T(1024)}, u32[]{:S(2)}) copy-start(f32[768]{0:T(1024)} %param.21) | copy-start | bytes 9220
  7.2 4.5 %copy-start.16 = (bf16[768,192]{0,1:T(8,128)(2,1)S(1)}, bf16[768,192]{0,1:T(8,128)(2,1)}, u32[]{:S(2)}) copy-start(bf16[768,192]{0,1:T(8,128)(2,1)} %param.17) | copy-start | bytes 884740
  7.2 4.8 %copy-start.18 = (bf16[768,192]{0,1:T(8,128)(2,1)S(1)}, bf16[768,192]{0,1:T(8,128)(2,1)}, u32[]{:S(2)}) copy-start(bf16[768,192]{0,1:T(8,128)(2,1)} %param.18) | copy-start | bytes 884740
  7.2 5.1 %copy-start.45 = (s32[1,4]{1,0:T(1,128)S(1)}, s32[1,4]{1,0:T(1,128)}, u32[]{:S(2)}) copy-start(s32[1,4]{1,0:T(1,128)} %param.16) | copy-start | bytes 52
  7.3 30.2 %all-gather.3.cloned.1.call-start = ((), (), s32[]{:S(2)}) async-start(), calls=%async_computation.7 | async-start | bytes 1966080 | tf_op jit(solution)/shard_map/all_gather | solution.py:111
  7.4 5.3 %copy-start.27 = (s32[128,128]{1,0:T(8,128)}, s32[128,128]{1,0:T(8,128)S(1)}, u32[]{:S(2)}) copy-start(s32[128,128]{1,0:T(8,128)S(1)} %compare_select_fusion) | copy-start | bytes 196612
  8.7 4.1 %copy-start.35 = (f32[128]{0:T(128)}, f32[128]{0:T(128)S(1)}, u32[]{:S(2)}) copy-start(f32[128]{0:T(128)S(1)} %add_rsqrt_fusion.1) | copy-start | bytes 1540
  10.1 3.8 %copy-start.6 = (bf16[192,768]{1,0:T(8,128)(2,1)S(1)}, bf16[192,768]{1,0:T(8,128)(2,1)}, u32[]{:S(2)}) copy-start(bf16[192,768]{1,0:T(8,128)(2,1)} %param.20) | copy-start | bytes 884740
  12.0 4.1 %copy-start.20 = (bf16[128,192]{0,1:T(8,128)(2,1)}, bf16[128,192]{0,1:T(8,128)(2,1)S(1)}, u32[]{:S(2)}) copy-start(bf16[128,192]{0,1:T(8,128)(2,1)S(1)} %convolution_convert_fusion.5) | copy-start | bytes 147460
  12.4 25.1 %copy-start.22 = (bf16[128,192]{0,1:T(8,128)(2,1)}, bf16[128,192]{0,1:T(8,128)(2,1)S(1)}, u32[]{:S(2)}) copy-start(bf16[128,192]{0,1:T(8,128)(2,1)S(1)} %convolution_convert_fusion.4) | copy-start | bytes 147460
  15.4 24.2 %copy-start.30 = (f32[768]{0:T(1024)S(1)}, f32[768]{0:T(1024)}, u32[]{:S(2)}) copy-start(f32[768]{0:T(1024)} %param.22) | copy-start | bytes 9220
  16.5 20.9 %copy-start.42 = (s32[256,1]{0,1:T(1,128)}, s32[256,1]{0,1:T(1,128)S(1)}, u32[]{:S(2)}) copy-start(s32[256,1]{0,1:T(1,128)S(1)} %compare_select_fusion.1) | copy-start | bytes 3076
  43.1 5.6 %copy-start.4 = (bf16[128,768]{1,0:T(8,128)(2,1)S(1)}, bf16[128,768]{1,0:T(8,128)(2,1)}, u32[]{:S(2)}) copy-start(bf16[128,768]{1,0:T(8,128)(2,1)} %param.27) | copy-start | bytes 589828
  43.1 26.3 %all-to-all-start = ((bf16[8,64,768]{2,1,0:T(8,128)(2,1)}), bf16[8,64,768]{2,1,0:T(8,128)(2,1)}, u32[]{:S(2)}, u32[]{:S(2)}) async-start(bf16[8,64,768]{2,1,0:T(8,128)(2,1)} %bitcast.14), calls=%async_computation | async-start | bytes 1572864 | tf_op jit(solution)/shard_map/all_to_all | solution.py:133
  69.4 4.4 %copy-start.44 = (bf16[1,768,768]{2,1,0:T(8,128)(2,1)S(1)}, bf16[1,768,768]{2,1,0:T(8,128)(2,1)}, u32[]{:S(2)}) copy-start(bf16[1,768,768]{2,1,0:T(8,128)(2,1)} %param.25) | copy-start | bytes 3538948
  69.4 24.3 %all-to-all-start.2 = ((bf16[8,64,768]{2,1,0:T(8,128)(2,1)}), bf16[8,64,768]{2,1,0:T(8,128)(2,1)}, u32[]{:S(2)}, u32[]{:S(2)}) async-start(bf16[8,64,768]{2,1,0:T(8,128)(2,1)} %bitcast.26), calls=%async_computation.2 | async-start | bytes 1572864 | tf_op jit(solution)/shard_map/all_to_all | solution.py:168
  73.8 32.6 %reduce-scatter.7.cloned.1.call-start = ((), (), s32[]{:S(2)}) async-start(), calls=%async_computation.8 | async-start | bytes 983040
  82.6 66.7 %reduce-scatter.9.cloned.1.call-start = ((), (), s32[]{:S(2)}) async-start(), calls=%async_computation.9 | async-start | bytes 1966080
  105.9 8.1 %copy-start.5 = (bf16[128,768]{1,0:T(8,128)(2,1)S(1)}, bf16[128,768]{1,0:T(8,128)(2,1)}, u32[]{:S(2)}) copy-start(bf16[128,768]{1,0:T(8,128)(2,1)} %param.27) | copy-start | bytes 589828
  105.9 8.9 %copy-start.43 = (s32[256,1]{0,1:T(1,128)S(1)}, s32[256,1]{0,1:T(1,128)}, u32[]{:S(2)}) copy-start(s32[256,1]{0,1:T(1,128)} %copy-done.42) | copy-start | bytes 3076
  108.5 14.4 %all-to-all-start.1 = ((bf16[8,64,192]{2,1,0:T(8,128)(2,1)}), bf16[8,64,192]{2,1,0:T(8,128)(2,1)S(1)}, u32[]{:S(2)}, u32[]{:S(2)}) async-start(bf16[8,64,192]{2,1,0:T(8,128)(2,1)} %copy.97), calls=%async_computation.1 | async-start | bytes 524288 | tf_op jit(solution)/shard_map/all_to_all | solution.py:143
  146.8 8.2 %copy-start.34 = (f32[128]{0:T(128)S(1)}, f32[128]{0:T(128)}, u32[]{:S(2)}) copy-start(f32[128]{0:T(128)} %copy-done.33) | copy-start | bytes 1540
  146.8 8.2 %copy-start.39 = (f32[128]{0:T(128)S(1)}, f32[128]{0:T(128)}, u32[]{:S(2)}) copy-start(f32[128]{0:T(128)} %copy-done.38) | copy-start | bytes 1540
  146.8 8.2 %copy-start.32 = (s32[128,2]{0,1:T(2,128)S(1)}, s32[128,2]{0,1:T(2,128)}, u32[]{:S(2)}) copy-start(s32[128,2]{0,1:T(2,128)} %param.15) | copy-start | bytes 3076
  151.5 13.1 %all-to-all-start.3 = ((bf16[8,64,192]{2,1,0:T(8,128)(2,1)}), bf16[8,64,192]{2,1,0:T(8,128)(2,1)S(1)}, u32[]{:S(2)}, u32[]{:S(2)}) async-start(bf16[8,64,192]{2,1,0:T(8,128)(2,1)} %copy.99), calls=%async_computation.3 | async-start | bytes 524288 | tf_op jit(solution)/shard_map/all_to_all | solution.py:187
  154.9 69.6 %all-reduce.7.cloned.1.call-start = ((), (), s32[]{:S(2)}) async-start(), calls=%async_computation.6 | async-start | bytes 393216 | tf_op jit(solution)/shard_map/psum | solution.py:243
  189.1 3.5 %copy-start.19 = (bf16[768,192]{0,1:T(8,128)(2,1)S(1)}, bf16[768,192]{0,1:T(8,128)(2,1)}, u32[]{:S(2)}) copy-start(bf16[768,192]{0,1:T(8,128)(2,1)} %param.18) | copy-start | bytes 884740
  193.9 146.4 %all-reduce.9.cloned.1.call-start = ((), (), s32[]{:S(2)}) async-start(), calls=%async_computation.10 | async-start | bytes 4718592 | tf_op jit(solution)/shard_map/psum | solution.py:251
  198.6 3.9 %copy-start.28 = (s32[128,128]{1,0:T(8,128)S(1)}, s32[128,128]{1,0:T(8,128)}, u32[]{:S(2)}) copy-start(s32[128,128]{1,0:T(8,128)} %copy-done.27) | copy-start | bytes 196612
  340.3 3.7 %copy-start.8 = (f32[192,768]{1,0:T(8,128)S(1)}, f32[192,768]{1,0:T(8,128)}, u32[]{:S(2)}) copy-start(f32[192,768]{1,0:T(8,128)} %get-tuple-element.44) | copy-start | bytes 1769476
  (27 other events, 52.0 us)
Sparse Core Ops, SparseCore 0:
  15.0 22.3 all-gather.2
  82.7 23.6 reduce-scatter.6
  109.7 33.9 reduce-scatter.8
  194.0 30.4 all-reduce.6
  229.4 110.8 all-reduce.8
